TPU v7x, 32 devices: a whole 2x2x4 slice. The times are simulated.
32 devices in a mesh: row: 4 (over z), col: 8 (over y, x, core).
Axes of the slice: x: 2, y: 2, z: 4, core: 2. Of those that a mesh axis runs over, the one named last changes fastest.
Arguments:
- coefficients: float32 [3, 7, 1024, 3072], P(None, None, 'col', 'row'), may hold values from -0.6 to 0.6
- basis_values: float32 [4, 4], replicated, may hold values from 0.05 to 1
- basis_slopes: float32 [4, 4], replicated, may hold values from -150 to 150
- band_offsets: int32 [4], replicated, may hold values from 0 to 3, as said below
Outputs:
- nonlinear_terms: float32 [3, 4, 1024, 3072], P(None, None, 'col', 'row')
Inputs may be any that keep to these rules, and one draw needn't show every extreme that they name: `band_offsets`: nondecreasing over the planes; the first is 0 and the last 3.
All inputs are finite; a program needn't handle non-finite values.
Results may differ from a plain program's by a relative error of at most 0.0095.
Values may be sent and summed in bfloat16 or wider, within the bound.
A program may use at most 128 MiB of HBM per device.

v0:
```python
import math

import jax
import jax.numpy as jnp
from jax import lax
from jax.sharding import PartitionSpec as P

stream_unit = 0.25
span_unit = 2.0 / 3.0


def collocation(offsets, weights, spline_total):
    band_width = weights.shape[1]
    selected = (
        jnp.arange(spline_total, dtype=jnp.int32)[None, None, :]
        == offsets[:, None, None] + jnp.arange(band_width, dtype=jnp.int32)[None, :, None]
    )
    return jnp.sum(jnp.where(selected, weights[:, :, None], 0.0), axis=1)


def signed_wave(mode_index, mode_total):
    signed = jnp.where(mode_index < mode_total // 2, mode_index, mode_index - mode_total)
    return signed.astype(jnp.float32) * span_unit


def vorticity(velocity, slopes, stream_wave, span_wave):
    real_part = velocity[:, 0].astype(jnp.float32)
    imag_part = velocity[:, 1].astype(jnp.float32)
    slope_real = slopes[:, 0].astype(jnp.float32)
    slope_imag = slopes[:, 1].astype(jnp.float32)
    reals = [
        -span_wave * imag_part[1] - slope_real[1],
        -(stream_wave * imag_part[2] - span_wave * imag_part[0]),
        slope_real[0] + stream_wave * imag_part[1],
    ]
    imags = [
        span_wave * real_part[1] - slope_imag[1],
        stream_wave * real_part[2] - span_wave * real_part[0],
        slope_imag[0] - stream_wave * real_part[1],
    ]
    return jnp.stack([jnp.stack([reals[k], imags[k]]) for k in range(3)]).astype(jnp.bfloat16)


def span_tables(mode_total, points):
    mode_index = jnp.arange(mode_total, dtype=jnp.int32)
    signed = jnp.where(mode_index < mode_total // 2, mode_index, mode_index - mode_total)
    point_index = jnp.arange(points, dtype=jnp.int32)
    angles = jnp.mod(signed[:, None] * point_index[None, :], points).astype(jnp.float32) * (
        2.0 * math.pi / points
    )
    cosines = jnp.cos(angles)
    sine_wave = jnp.sin(angles)
    return (
        cosines.astype(jnp.bfloat16),
        (sine_wave - cosines).astype(jnp.bfloat16),
        (cosines + sine_wave).astype(jnp.bfloat16),
    )


def stream_tables(mode_total, points):
    mode_index = jnp.arange(mode_total, dtype=jnp.int32)
    point_index = jnp.arange(points, dtype=jnp.int32)
    angles = jnp.mod(mode_index[:, None] * point_index[None, :], points).astype(jnp.float32) * (
        2.0 * math.pi / points
    )
    forward_table = jnp.stack([jnp.cos(angles), -jnp.sin(angles)]).astype(jnp.bfloat16)
    weight = jnp.where(mode_index == 0, 1.0, 2.0).astype(jnp.float32)
    inverse_table = (forward_table.astype(jnp.float32) * weight[None, :, None]).astype(jnp.bfloat16)
    return (forward_table, inverse_table)


def contract(left, table, form):
    return jnp.einsum(form, left, table, preferred_element_type=jnp.float32)


def inverse_span(fields, cosine_table, minus_table, plus_table):
    real_part = fields[:, 0]
    imag_part = fields[:, 1]
    summed = (real_part.astype(jnp.float32) + imag_part.astype(jnp.float32)).astype(jnp.bfloat16)
    common = contract(summed, cosine_table, "...q,qz->...z")
    real_out = common - contract(imag_part, plus_table, "...q,qz->...z")
    imag_out = common + contract(real_part, minus_table, "...q,qz->...z")
    return jnp.stack([real_out, imag_out], axis=1).astype(jnp.bfloat16)


def forward_span(spectral_x, cosine_table, minus_table, plus_table):
    real_part = spectral_x[:, 0]
    imag_part = spectral_x[:, 1]
    summed = (real_part.astype(jnp.float32) + imag_part.astype(jnp.float32)).astype(jnp.bfloat16)
    common = contract(summed, cosine_table, "...z,qz->...q")
    real_out = common + contract(imag_part, minus_table, "...z,qz->...q")
    imag_out = common - contract(real_part, plus_table, "...z,qz->...q")
    return jnp.stack([real_out, imag_out], axis=1)


def cross_product(physical):
    flow_part = physical[:3]
    twist_part = physical[3:]
    return jnp.stack(
        [
            flow_part[1] * twist_part[2] - flow_part[2] * twist_part[1],
            flow_part[2] * twist_part[0] - flow_part[0] * twist_part[2],
            flow_part[0] * twist_part[1] - flow_part[1] * twist_part[0],
        ]
    ).astype(jnp.bfloat16)


def on_device(coefficients, basis_values, basis_slopes, band_offsets):
    row_count = lax.axis_size("row")
    col_count = lax.axis_size("col")
    spline_total = coefficients.shape[1]
    stream_local = coefficients.shape[2]
    span_local = coefficients.shape[3] // 2
    split_coefficients = jnp.moveaxis(
        coefficients.reshape(3, spline_total, stream_local, span_local, 2), 4, 1
    )
    stream_modes = stream_local * col_count
    span_modes = span_local * row_count
    span_points = 3 * span_modes // 2
    stream_points = 3 * stream_modes
    value_map = collocation(band_offsets, basis_values, spline_total)
    slope_map = collocation(band_offsets, basis_slopes, spline_total)
    velocity = jnp.einsum(
        "js,cpsxz->cpjxz", value_map, split_coefficients, precision=lax.Precision.HIGHEST
    ).astype(jnp.bfloat16)
    slopes = jnp.einsum(
        "js,cpsxz->cpjxz", slope_map, split_coefficients[0::2], precision=lax.Precision.HIGHEST
    ).astype(jnp.bfloat16)
    stream_index = lax.axis_index("col") * stream_local + jnp.arange(stream_local, dtype=jnp.int32)
    stream_wave = (stream_index.astype(jnp.float32) * stream_unit)[:, None]
    span_index = lax.axis_index("row") * span_local + jnp.arange(span_local, dtype=jnp.int32)
    vortex = vorticity(velocity, slopes, stream_wave, signed_wave(span_index, span_modes))
    fields = jnp.concatenate([velocity, vortex], axis=0)
    spectral = lax.all_to_all(fields, "row", split_axis=2, concat_axis=4, tiled=True)
    cosine_table, minus_table, plus_table = span_tables(span_modes, span_points)
    span_grid = inverse_span(spectral, cosine_table, minus_table, plus_table)
    forward_table, inverse_table = stream_tables(stream_modes, stream_points)
    padded_local = stream_local + stream_local // 2
    padded = jnp.pad(span_grid, ((0, 0), (0, 0), (0, 0), (0, stream_local // 2), (0, 0)))
    blocked_table = inverse_table.reshape(2, col_count, stream_local, stream_points)
    padded_table = jnp.pad(
        blocked_table, ((0, 0), (0, 0), (0, padded_local - stream_local), (0, 0))
    ).reshape(2, col_count * padded_local, stream_points)
    physical = contract(
        lax.all_to_all(padded, "col", split_axis=4, concat_axis=3, tiled=True),
        padded_table,
        "fpymz,pmw->fyzw",
    )
    products = cross_product(physical)
    spectral_x = contract(products, forward_table, "cyzw,pmw->cpymz").astype(jnp.bfloat16)
    norm_factor = 1.0 / (stream_points * span_points)
    spectrum = (
        forward_span(
            lax.all_to_all(spectral_x, "col", split_axis=3, concat_axis=4, tiled=True),
            cosine_table,
            minus_table,
            plus_table,
        )
        * norm_factor
    )
    planes = lax.all_to_all(spectrum, "row", split_axis=4, concat_axis=2, tiled=True)
    plane_count = planes.shape[2]
    return jnp.moveaxis(planes, 1, 4).reshape(3, plane_count, stream_local, 2 * span_local)


def solution(mesh):
    placed = (P(None, None, "col", "row"), P(), P(), P())
    return jax.shard_map(
        on_device,
        mesh=mesh,
        in_specs=placed,
        out_specs=P(None, None, "col", "row"),
        check_vma=False,
    )
```

profile of v0, /device:TPU:0, one launch (start us, length us, event | category | flops | bytes accessed | tf_op | source)
XLA Modules:
  0.0 1055.5 jit_solution(4404840599084937016)
XLA Ops:
  0.0 0.7 iota_add_fusion
  0.7 8.9 copy.60
  9.6 11.5 %copy.61 = f32[3,7,128,384,2]{3,1,2,4,0:T(8,128)} copy(f32[3,7,128,384,2]{2,4,3,1,0:T(2,128)} %bitcast.270) | data formatting | bytes 16515072 | tf_op jit(solution)/shard_map/reshape | solution.py:115
  21.2 7.8 fusion.71
  29.5 9.0 convert_bitcast_fusion.1
  39.1 1.5 fusion.90
  42.3 4.7 pad_maximum_fusion.1
  47.0 3.1 copy.62
  50.2 6.3 all-to-all-start
  56.5 104.8 %all-to-all-done = bf16[6,2,4,128,384]{4,3,1,0,2:T(8,128)(2,1)} async-done(((bf16[6,2,4,128,384]{4,3,1,0,2:T(8,128)(2,1)}), bf16[6,2,4,128,384]{4,3,1,0,2:T(8,128)(2,1)}, u32[]{:S(2)}, u32[]{:S(2)}) %all-to-all-start) | async-done | bytes 4718624 | tf_op jit(solution)/shard_map/all_to_all | solution.py:134
  161.2 8.2 copy.63
  169.4 8.8 all_to_all.53
  178.2 2.1 slice_bitcast_fusion.23
  180.2 1.0 copy-done.1
  181.5 0.7 add_convert_fusion.13
  182.2 58.4 %fusion.26 = f32[6,128,2304]{2,1,0:T(8,128)S(1)} fusion(s32[1536]{0:T(1024)S(1)} %compare_select_fusion, bf16[6,128,1536]{2,1,0:T(8,128)(2,1)S(1)} %add_convert_fusion.13), kind=kOutput, calls=%fused_computation.44 | convolution fusion | flops 5471207424 | bytes 9443328 | tf_op jit(solution)/shard_map/...q,qz->...z/dot_general | solution.py:73
  240.6 63.4 %fusion.49 = bf16[6,1,1,128,2304]{4,3,0,2,1:T(8,128)(2,1)S(1)} fusion(f32[6,128,2304]{2,1,0:T(8,128)S(1)} %fusion.26, s32[1536]{0:T(1024)S(1)} %compare_select_fusion, bf16[6,128,1536]{2,1,0:T(8,128)(2,1)S(1)} %slice_bitcast_fusion.23), kind=kOutput, calls=%fused_computation.60 | convolution fusion | flops 5478285312 | bytes 12982272 | tf_op jit(solution)/shard_map/...q,qz->...z/dot_general | solution.py:73
  304.0 63.1 %fusion.46 = bf16[6,1,1,128,2304]{4,3,0,2,1:T(8,128)(2,1)S(1)} fusion(f32[6,128,2304]{2,1,0:T(8,128)S(1)} %fusion.26, s32[1536]{0:T(1024)S(1)} %compare_select_fusion, bf16[6,128,1536]{2,1,0:T(8,128)(2,1)S(1)} %slice_bitcast_fusion.22), kind=kOutput, calls=%fused_computation.59 | convolution fusion | flops 5478285312 | bytes 12982272 | tf_op jit(solution)/shard_map/...q,qz->...z/dot_general | solution.py:73
  367.1 3.5 pad_maximum_fusion
  370.6 18.1 %copy.82 = bf16[6,2,1,128,2304]{3,1,2,0,4:T(2,128)(2,1)} copy(bf16[6,2,1,128,2304]{4,3,0,2,1:T(8,128)(2,1)} %pad_maximum_fusion) | data formatting | bytes 14155776
  388.8 11.9 %pad.8.clone = bf16[6,2,1,192,2304]{3,1,2,0,4:T(2,128)(2,1)} pad(bf16[6,2,1,128,2304]{3,1,2,0,4:T(2,128)(2,1)} %copy.82, bf16[]{:T(256)} %constant.62.clone.1), padding=0_0x0_0x0_0x0_64x0_0 | pad | bytes 17694722 | tf_op jit(solution)/shard_map/jit(_pad)/pad | solution.py:139
  400.7 5.7 all-to-all-start.1
  406.4 52.9 %cosine_convert_fusion = (bf16[1,8,128,3072]{3,2,1,0:T(8,128)(2,1)S(1)}, bf16[1,8,128,3072]{3,2,1,0:T(8,128)(2,1)S(1)}) fusion(s32[8,128]{1,0:T(8,128)S(1)} %multiply_add_fusion), kind=kLoop, calls=%fused_computation.25 | loop fusion | flops 37748736 | bytes 12587008 | tf_op jit(solution)/shard_map/convert.3
  459.3 2.5 multiply_convert_fusion
  461.8 10.0 pad.9
  471.8 52.8 %negate_convert_fusion.1 = (bf16[1,1024,3072]{2,1,0:T(8,128)(2,1)}, bf16[1,1024,3072]{2,1,0:T(8,128)(2,1)}) fusion(), kind=kLoop, calls=%fused_computation.29 | loop fusion | flops 37748736 | bytes 12582912 | tf_op jit(solution)/shard_map/convert.22
  524.6 37.6 %all-to-all-done.1 = bf16[6,2,1,192,2304]{3,1,2,0,4:T(2,128)(2,1)} async-done(((bf16[6,2,1,192,2304]{3,1,2,0,4:T(2,128)(2,1)}), bf16[6,2,1,192,2304]{3,1,2,0,4:T(2,128)(2,1)}, u32[]{:S(2)}, u32[]{:S(2)}) %all-to-all-start.1) | async-done | bytes 10616864 | tf_op jit(solution)/shard_map/all_to_all | solution.py:145
  562.2 14.2 %copy.84 = bf16[6,2,1,192,8,288]{3,4,5,1,0,2:T(8,128)(2,1)} copy(bf16[6,2,1,192,8,288]{3,1,0,5,4,2:T(2,128)(2,1)} %bitcast.32) | data formatting | bytes 21233664 | tf_op jit(solution)/shard_map/all_to_all | solution.py:145
  576.5 22.3 %reshape.332 = bf16[6,2,1536,288]{2,3,1,0:T(8,128)(2,1)} reshape(bf16[6,2,1,8,192,288]{4,3,5,1,0,2:T(8,128)(2,1)} %bitcast.269) | data formatting | bytes 21233664 | tf_op jit(solution)/shard_map/reshape.12
  598.7 38.8 %convolution_bitcast_fusion = f32[6,288,3072]{2,1,0:T(8,128)S(1)} fusion(bf16[6,2,1536,288]{2,3,1,0:T(8,128)(2,1)} %reshape.332, bf16[2,1536,3072,1]{2,1,0,3:T(8,128)(2,1)} %bitcast.274), kind=kOutput, calls=%fused_computation.36 | convolution fusion | flops 32614907904 | bytes 50724864 | tf_op jit(solution)/shard_map/fpymz,pmw->fyzw/dot_general | solution.py:73
  637.6 5.1 subtract_convert_fusion.4
  642.7 15.7 %convert_bitcast_fusion = bf16[3,2,1,1024,288]{3,4,0,1,2:T(8,128)(2,1)S(1)} fusion(bf16[1,288,3072]{2,1,0:T(8,128)(2,1)} %get-tuple-element.9, bf16[1,288,3072]{2,1,0:T(8,128)(2,1)} %get-tuple-element.8, bf16[1,288,3072]{2,1,0:T(8,128)(2,1)} %get-tuple-element.7, bf16[1,1024,3072]{2,1,0:T(8,128)(2,1)} %get-tuple-element.29, ...), kind=kOutput, calls=%fused_computation.62 | convolution fusion | flops 10914496512 | bytes 21430272 | tf_op jit(solution)/shard_map/cyzw,pmw->cpymz/dot_general | solution.py:73
  658.4 8.3 copy.66
  666.7 59.4 %all_to_all.69 = bf16[3,2,1,1024,288]{4,1,2,0,3:T(2,128)(2,1)} all-to-all(bf16[3,2,1,1024,288]{4,1,2,0,3:T(2,128)(2,1)} %copy.66), channel_id=1, replica_groups=mesh['row'=4,'col'=8] {'col'}, dimensions={3} | all-to-all | bytes 7077888 | tf_op jit(solution)/shard_map/all_to_all | solution.py:154
  726.1 11.0 %copy.79 = bf16[3,2,1,8,128,288]{4,5,3,1,0,2:T(8,128)(2,1)S(1)} copy(bf16[3,2,1,8,128,288]{5,1,0,4,3,2:T(2,128)(2,1)} %bitcast.277) | data formatting | bytes 7077888 | tf_op jit(solution)/shard_map/all_to_all | solution.py:154
  737.0 1.4 fusion.149
  738.4 1.3 fusion.151
  739.7 2.0 fusion.118
  741.7 2.6 copy.80
  744.4 2.6 copy.81
  747.4 55.3 %fusion.24 = f32[3,128,1536]{2,1,0:T(8,128)S(1)} fusion(s32[1536]{0:T(1024)S(1)} %copy-done.5, bf16[3,128,2304]{2,1,0:T(8,128)(2,1)S(1)} %add_convert_fusion.12), kind=kOutput, calls=%fused_computation.43 | convolution fusion | flops 2753298432 | bytes 4134912 | tf_op jit(solution)/shard_map/...z,qz->...q/dot_general | solution.py:73
  802.8 61.4 %fusion.61 = f32[3,1,1,128,1536]{4,3,0,2,1:T(8,128)S(1)} fusion(f32[3,128,1536]{2,1,0:T(8,128)S(1)} %fusion.24, s32[1536]{0:T(1024)S(1)} %copy-done.5, bf16[3,128,2304]{1,2,0:T(8,128)(2,1)S(1)} %copy-done.3), kind=kOutput, calls=%fused_computation.69 | convolution fusion | flops 2757427200 | bytes 6494208 | tf_op jit(solution)/shard_map/...z,qz->...q/dot_general | solution.py:73
  864.2 61.5 %fusion.58 = f32[3,1,1,128,1536]{4,3,0,2,1:T(8,128)S(1)} fusion(f32[3,128,1536]{2,1,0:T(8,128)S(1)} %fusion.24, s32[1536]{0:T(1024)S(1)} %copy-done.5, bf16[3,128,2304]{1,2,0:T(8,128)(2,1)S(1)} %copy-done.2), kind=kOutput, calls=%fused_computation.68 | convolution fusion | flops 2757427200 | bytes 6494208 | tf_op jit(solution)/shard_map/...z,qz->...q/dot_general | solution.py:73
  925.8 3.0 maximum_multiply_fusion
  928.8 8.1 copy.71
  936.9 107.8 %all_to_all.70 = f32[3,2,1,128,1536]{3,1,2,0,4:T(2,128)S(1)} all-to-all(f32[3,2,1,128,1536]{3,1,2,0,4:T(2,128)} %copy.71), channel_id=1, replica_groups=mesh['row'=4,'col'=8] {'row'}, dimensions={4} | all-to-all | bytes 9437184 | tf_op jit(solution)/shard_map/all_to_all | solution.py:161
  1044.7 4.3 copy.72
  1049.0 6.0 copy.73
  (28 shorter events, 3.5 us)
Async XLA Ops:
  9.6 11.5 %copy-start.6 = (f32[4,4]{1,0:T(4,128)S(1)}, f32[4,4]{1,0:T(4,128)}, u32[]{:S(2)}) copy-start(f32[4,4]{1,0:T(4,128)} %param.5) | copy-start | bytes 196
  9.6 11.5 %copy-start.7 = (f32[4,4]{1,0:T(4,128)S(1)}, f32[4,4]{1,0:T(4,128)}, u32[]{:S(2)}) copy-start(f32[4,4]{1,0:T(4,128)} %param.6) | copy-start | bytes 196
  21.2 8.2 copy-start
  50.2 111.1 %all-to-all-start = ((bf16[6,2,4,128,384]{4,3,1,0,2:T(8,128)(2,1)}), bf16[6,2,4,128,384]{4,3,1,0,2:T(8,128)(2,1)}, u32[]{:S(2)}, u32[]{:S(2)}) async-start(bf16[6,2,4,128,384]{4,3,1,0,2:T(8,128)(2,1)} %copy.62), calls=%async_computation | async-start | bytes 9437184 | tf_op jit(solution)/shard_map/all_to_all | solution.py:134
  56.5 247.5 %copy-start.4 = (s32[1536]{0:T(1024)}, s32[1536]{0:T(1024)S(1)}, u32[]{:S(2)}) copy-start(s32[1536]{0:T(1024)S(1)} %compare_select_fusion) | copy-start | bytes 18436
  178.2 3.0 copy-start.1
  400.7 161.5 %all-to-all-start.1 = ((bf16[6,2,1,192,2304]{3,1,2,0,4:T(2,128)(2,1)}), bf16[6,2,1,192,2304]{3,1,2,0,4:T(2,128)(2,1)}, u32[]{:S(2)}, u32[]{:S(2)}) async-start(bf16[6,2,1,192,2304]{3,1,2,0,4:T(2,128)(2,1)} %pad.8.clone), calls=%async_computation.1 | async-start | bytes 28311552 | tf_op jit(solution)/shard_map/all_to_all | solution.py:145
  741.7 5.7 copy-start.5
  747.4 55.3 %copy-start.3 = (bf16[3,128,2304]{1,2,0:T(8,128)(2,1)S(1)}, bf16[3,128,2304]{1,2,0:T(8,128)(2,1)}, u32[]{:S(2)}) copy-start(bf16[3,128,2304]{1,2,0:T(8,128)(2,1)} %fusion.151) | copy-start | bytes 5308420
  802.8 61.5 %copy-start.2 = (bf16[3,128,2304]{1,2,0:T(8,128)(2,1)S(1)}, bf16[3,128,2304]{1,2,0:T(8,128)(2,1)}, u32[]{:S(2)}) copy-start(bf16[3,128,2304]{1,2,0:T(8,128)(2,1)} %fusion.149) | copy-start | bytes 5308420
where the time goes:
time: 1070 us; the launch traced here: 1060 us
  matrix products  435 us (41%)
  local copies, waits for them, and re-layouts  168 us (16%)
  blocking collectives  167 us (16%)
  waiting for transfers between devices  142 us (13%)
  other arithmetic  131 us (12%)
  starting transfers between devices  12 us (1%)
    dot_general x8, matrix products, contract(): return jnp.einsum(form, left, table, preferred_element_type=jnp.float32)  418 us
    another operation x4, other arithmetic  112 us
    all_to_all x1, blocking collectives, on_device(): lax.all_to_all(spectrum, 'row', split_axis=4, concat_axis=2, tiled=True)  108 us
    all_to_all x1, waiting for transfers between devices, on_device(): lax.all_to_all(fields, 'row', split_axis=2, concat_axis=4, tiled=True)  105 us
    all_to_all x1, blocking collectives, on_device(): lax.all_to_all(spectral_x, 'col', split_axis=3, concat_axis=4, tiled=True)  59.4 us
    all_to_all x1, waiting for transfers between devices, on_device(): lax.all_to_all(padded, 'col', split_axis=4, concat_axis=3, tiled=True)  37.6 us
    unnamed x20, local copies, waits for them, and re-layouts  33.3 us
    another operation x1, local copies, waits for them, and re-layouts  22.3 us
  transfers between devices with their start and end apart: 2, of which 2 were waited for; matrix products, arithmetic and copies ran while one was open for 11% of the time, Pallas kernels for 0%

commit v1 on v0

v1 whole, which is shorter than its diff:
```python
import functools
import math

import jax
import jax.numpy as jnp
import ml_dtypes
import numpy as np
from jax import lax
from jax.experimental import pallas as pl
from jax.experimental.pallas import tpu as pltpu
from jax.sharding import PartitionSpec as P

stream_unit = 0.25
span_unit = 2.0 / 3.0
VMEM_LIMIT = 56 * 1024 * 1024
BF = jnp.bfloat16
F32 = jnp.float32


def span_tables(mode_total, points):
    mode = np.arange(mode_total)
    signed = np.where(mode < mode_total // 2, mode, mode - mode_total)
    odd = 2 * np.arange(points // 2) + 1
    angle = np.mod(odd[:, None] * signed[None, :], 2 * points) * (math.pi / points)
    return np.cos(angle).astype(ml_dtypes.bfloat16), np.sin(angle).astype(ml_dtypes.bfloat16)


def stream_tables(mode_total, points):
    mode = np.arange(mode_total)
    odd = 2 * np.arange(points // 2) + 1
    angle = np.mod(mode[:, None] * odd[None, :], 2 * points) * (math.pi / points)
    return np.cos(angle).astype(ml_dtypes.bfloat16), (-np.sin(angle)).astype(ml_dtypes.bfloat16)


def split_table(count):
    table = np.zeros((2, count, 2 * count), ml_dtypes.bfloat16)
    index = np.arange(count)
    table[0, index, 2 * index] = 1
    table[1, index, 2 * index + 1] = 1
    return table.reshape(2 * count, 2 * count)


def dot(left, right):
    return jnp.dot(left, right, preferred_element_type=F32)


def collocate_kernel(values, slopes, offsets, coef, first, second):
    planes = values.shape[0]
    for j in range(planes):
        base = offsets[j]

        def total(weights, c):
            return sum(
                weights[j, t] * coef[c, base + t] for t in range(weights.shape[1])
            ).astype(BF)

        first[j, 0] = total(values, 0)
        first[j, 1] = total(values, 2)
        second[j, 0] = total(values, 1)
        second[j, 1] = total(slopes, 0)
        second[j, 2] = total(slopes, 2)


def collocate(coefficients, values, slopes, offsets, rows):
    _, splines, stream_local, width = coefficients.shape
    planes = values.shape[0]
    smem = pl.BlockSpec(memory_space=pltpu.SMEM)
    return pl.pallas_call(
        collocate_kernel,
        grid=(stream_local // rows,),
        in_specs=[smem, smem, smem, pl.BlockSpec((3, splines, rows, width), lambda i: (0, 0, i, 0))],
        out_specs=[
            pl.BlockSpec((planes, 2, rows, width), lambda i: (0, 0, i, 0)),
            pl.BlockSpec((planes, 3, rows, width), lambda i: (0, 0, i, 0)),
        ],
        out_shape=[
            jax.ShapeDtypeStruct((planes, 2, stream_local, width), BF),
            jax.ShapeDtypeStruct((planes, 3, stream_local, width), BF),
        ],
        compiler_params=pltpu.CompilerParams(vmem_limit_bytes=VMEM_LIMIT),
        name="collocate",
    )(values, slopes, offsets, coefficients)


def inverse_kernel(group, span_modes, x, stream_wave, split, cosine, sine, out, modes):
    rows, sent, stream_local, width = x.shape
    half = width // 2

    @pl.when(pl.program_id(0) == 0)
    def _():
        wave_x = stream_wave[...]

        def body(r, carry):
            flat = x[r].reshape(sent * stream_local, width)
            parts = lax.dot_general(
                split[...], flat, (((1,), (1,)), ((), ())), preferred_element_type=F32
            )
            field = lambda k: (
                parts[:half, k * stream_local : (k + 1) * stream_local],
                parts[half:, k * stream_local : (k + 1) * stream_local],
            )
            mode = r * half + lax.broadcasted_iota(jnp.int32, (half, stream_local), 0)
            signed = jnp.where(mode < span_modes // 2, mode, mode - span_modes)
            wave_z = signed.astype(F32) * span_unit
            if group == 0:
                (ur, ui), (wr, wi) = field(0), field(1)
                fields = [
                    (ur, ui),
                    (wr, wi),
                    (-(wave_x * wi - wave_z * ui), wave_x * wr - wave_z * ur),
                ]
            else:
                (vr, vi), (sur, sui), (swr, swi) = field(0), field(1), field(2)
                fields = [
                    (vr, vi),
                    (-wave_z * vi - swr, wave_z * vr - swi),
                    (sur + wave_x * vi, sui - wave_x * vr),
                ]
            here = pl.ds(pl.multiple_of(r * half, 16), half)
            for f in range(3):
                for p in range(2):
                    at = (p * 3 + f) * stream_local
                    modes[here, at : at + stream_local] = fields[f][p].astype(BF)
            return carry

        lax.fori_loop(0, rows, body, 0)

    by_cosine = dot(cosine[...], modes[...])
    by_sine = dot(sine[...], modes[...])
    part = 3 * stream_local
    pairs = [
        (by_cosine[:, :part], -by_sine[:, part:]),
        (by_cosine[:, part:], by_sine[:, :part]),
    ]
    block = out.shape[3] // 2
    for p, (even, odd) in enumerate(pairs):
        plus = (even + odd).astype(BF)
        minus = (even - odd).astype(BF)
        for d in range(out.shape[0]):
            for f in range(3):
                lanes = slice(f * stream_local, (f + 1) * stream_local)
                out[d, f, p, :block] = plus[d * block : (d + 1) * block, lanes]
                out[d, f, p, block:] = minus[d * block : (d + 1) * block, lanes]


def inverse_span(group, x, stream_wave, split, cosine, sine, col_count):
    rows, sent, stream_local, width = x.shape
    half_points, span_modes = cosine.shape
    block = half_points // col_count
    step = 2
    whole = lambda a: pl.BlockSpec(a.shape, lambda i: (0,) * a.ndim)
    table = pl.BlockSpec((step * block, span_modes), lambda i: (i, 0))
    return pl.pallas_call(
        functools.partial(inverse_kernel, group, span_modes),
        grid=(col_count // step,),
        in_specs=[whole(x), whole(stream_wave), whole(split), table, table],
        out_specs=pl.BlockSpec(
            (step, 3, 2, 2 * block, stream_local), lambda i: (i, 0, 0, 0, 0)
        ),
        out_shape=jax.ShapeDtypeStruct((col_count, 3, 2, 2 * block, stream_local), BF),
        scratch_shapes=[pltpu.VMEM((span_modes, 6 * stream_local), BF)],
        compiler_params=pltpu.CompilerParams(vmem_limit_bytes=VMEM_LIMIT),
        cost_estimate=pl.CostEstimate(
            flops=2 * 12 * stream_local * span_modes * half_points,
            bytes_accessed=4 * half_points * span_modes + 4 * x.size,
            transcendentals=0,
        ),
        name="inverse_span",
    )(x, stream_wave, split, cosine, sine)


def product_kernel(chunk, ga, gb, wave_c, wave_s, back_c, back_s, o0, o1, o2, reals, imags, acc_re, acc_im):
    cols, _, _, _, hb, lanes = ga.shape
    per = 2 * hb
    for g, ref in enumerate((ga, gb)):
        for f in range(3):
            row = (g * 3 + f) * per
            for d in range(cols):
                at = slice(d * lanes, (d + 1) * lanes)
                for s in range(2):
                    reals[row + s * hb : row + (s + 1) * hb, at] = ref[d, f, 0, s]
                    imags[row + s * hb : row + (s + 1) * hb, at] = ref[d, f, 1, s]
    points = wave_c.shape[1]
    for b in range(points // chunk):
        xs = slice(b * chunk, (b + 1) * chunk)
        even = dot(reals[...], wave_c[:, xs])
        odd = dot(imags[...], wave_s[:, xs])
        products = []
        for phys in (even + odd, even - odd):
            u, w, wy, v, wx, wz = [phys[k * per : (k + 1) * per] for k in range(6)]
            products.append((v * wz - w * wy, w * wx - u * wz, u * wy - v * wx))
        sums = []
        diffs = []
        for c in range(3):
            total = products[0][c] + products[1][c]
            gap = products[0][c] - products[1][c]
            sums += [total[:hb] + total[hb:], total[:hb] - total[hb:]]
            diffs += [gap[:hb] + gap[hb:], gap[:hb] - gap[hb:]]
        re = dot(jnp.concatenate(sums, axis=0).astype(BF), back_c[xs, :])
        im = dot(jnp.concatenate(diffs, axis=0).astype(BF), back_s[xs, :])
        if b == 0:
            acc_re[...] = re
            acc_im[...] = im
        else:
            acc_re[...] += re
            acc_im[...] += im
    for c, out in enumerate((o0, o1, o2)):
        for s in range(2):
            row = (c * 2 + s) * hb
            for d in range(cols):
                at = slice(d * lanes, (d + 1) * lanes)
                out[d, 0, s] = acc_re[row : row + hb, at].astype(BF)
                out[d, 1, s] = acc_im[row : row + hb, at].astype(BF)


def products(ga, gb, tables, hb, chunk):
    cols, _, _, points, lanes = ga.shape
    half = points // 2
    shape = (cols, 3, 2, 2, half, lanes)
    ga, gb = ga.reshape(shape), gb.reshape(shape)
    modes = cols * lanes
    spec = pl.BlockSpec((cols, 3, 2, 2, hb, lanes), lambda i: (0, 0, 0, 0, i, 0))
    out_spec = pl.BlockSpec((cols, 2, 2, hb, lanes), lambda i: (0, 0, 0, i, 0))
    whole = lambda a: pl.BlockSpec(a.shape, lambda i: (0, 0), pipeline_mode=pl.Buffered(1))
    stream_half = tables[0].shape[1]
    return pl.pallas_call(
        functools.partial(product_kernel, chunk),
        grid=(half // hb,),
        in_specs=[spec, spec] + [whole(t) for t in tables],
        out_specs=[out_spec] * 3,
        out_shape=[jax.ShapeDtypeStruct((cols, 2, 2, half, lanes), BF)] * 3,
        scratch_shapes=[
            pltpu.VMEM((12 * hb, modes), BF),
            pltpu.VMEM((12 * hb, modes), BF),
            pltpu.VMEM((6 * hb, modes), F32),
            pltpu.VMEM((6 * hb, modes), F32),
        ],
        compiler_params=pltpu.CompilerParams(vmem_limit_bytes=VMEM_LIMIT),
        cost_estimate=pl.CostEstimate(
            flops=2 * 36 * half * modes * stream_half,
            bytes_accessed=8 * modes * stream_half + 36 * 2 * points * modes,
            transcendentals=0,
        ),
        name="products",
    )(ga, gb, *tables)


def forward_kernel(norm, spectral, split, cosine, sine, out, plus, minus):
    cols, _, _, block, lanes = spectral.shape

    @pl.when(pl.program_id(0) == 0)
    def _():
        for d in range(cols):
            here = slice(d * block, (d + 1) * block)
            for p in range(2):
                at = slice(p * lanes, (p + 1) * lanes)
                plus[here, at] = spectral[d, p, 0]
                minus[here, at] = spectral[d, p, 1]

    by_cosine = dot(cosine[...], plus[...])
    by_sine = dot(sine[...], minus[...])
    re = (by_cosine[:, :lanes] + by_sine[:, lanes:]) * norm
    im = (by_cosine[:, lanes:] - by_sine[:, :lanes]) * norm
    parts = jnp.concatenate([re, im], axis=0).astype(BF)
    out[0] = lax.dot_general(
        parts, split[...], (((0,), (0,)), ((), ())), preferred_element_type=F32
    ).astype(BF)


def forward_span(spectral, split, cosine, sine, norm, row_count):
    cols, _, _, block, lanes = spectral.shape
    span_modes, half_points = cosine.shape
    width = 2 * span_modes // row_count
    whole = lambda a: pl.BlockSpec(a.shape, lambda i: (0,) * a.ndim)
    table = pl.BlockSpec((width // 2, half_points), lambda i: (i, 0))
    return pl.pallas_call(
        functools.partial(forward_kernel, norm),
        grid=(row_count,),
        in_specs=[whole(spectral), whole(split), table, table],
        out_specs=pl.BlockSpec((1, lanes, width), lambda i: (i, 0, 0)),
        out_shape=jax.ShapeDtypeStruct((row_count, lanes, width), BF),
        scratch_shapes=[pltpu.VMEM((half_points, 2 * lanes), BF)] * 2,
        compiler_params=pltpu.CompilerParams(vmem_limit_bytes=VMEM_LIMIT),
        cost_estimate=pl.CostEstimate(
            flops=2 * 4 * lanes * span_modes * half_points,
            bytes_accessed=4 * half_points * span_modes + 4 * spectral.size,
            transcendentals=0,
        ),
        name="forward_span",
    )(spectral, split, cosine, sine)


def exchange(x, axis):
    return lax.all_to_all(x, axis, split_axis=0, concat_axis=0, tiled=True)


def on_device(coefficients, basis_values, basis_slopes, band_offsets):
    row_count = lax.axis_size("row")
    col_count = lax.axis_size("col")
    stream_local = coefficients.shape[2]
    span_local = coefficients.shape[3] // 2
    stream_modes = stream_local * col_count
    span_modes = span_local * row_count
    span_points = 3 * span_modes // 2
    stream_points = 3 * stream_modes
    cosine, sine = span_tables(span_modes, span_points)
    wave_c, wave_s = stream_tables(stream_modes, stream_points)
    weight = np.where(np.arange(stream_modes) == 0, 1.0, 2.0)[:, None].astype(ml_dtypes.bfloat16)
    stream = [wave_c * weight, wave_s * weight, wave_c.T, wave_s.T]
    stream = [jnp.asarray(np.ascontiguousarray(t)) for t in stream]
    split = jnp.asarray(split_table(span_local))
    span = jnp.asarray(cosine), jnp.asarray(sine)
    back = jnp.asarray(np.ascontiguousarray(cosine.T)), jnp.asarray(np.ascontiguousarray(sine.T))
    norm = 1.0 / (stream_points * span_points)

    stream_index = lax.axis_index("col") * stream_local + jnp.arange(stream_local, dtype=jnp.int32)
    stream_wave = (stream_index.astype(F32) * stream_unit)[None, :]

    sent = collocate(coefficients, basis_values, basis_slopes, band_offsets, 32)
    grids = []
    for group in range(2):
        modes = exchange(sent[group], "row")
        grid = inverse_span(group, modes, stream_wave, split, *span, col_count)
        grids.append(exchange(grid, "col"))
    half = span_points // 2 // col_count
    terms = products(*grids, stream, 48 if half % 48 == 0 else half, 512)
    results = []
    for term in terms:
        spectrum = forward_span(exchange(term, "col"), split, *back, norm, row_count)
        results.append(exchange(spectrum, "row"))
    return jnp.stack(results).astype(F32)


def solution(mesh):
    placed = (P(None, None, "col", "row"), P(), P(), P())
    return jax.shard_map(
        on_device,
        mesh=mesh,
        in_specs=placed,
        out_specs=P(None, None, "col", "row"),
        check_vma=False,
    )
```

time: 1070 us -> 360 us (0.34); the launches traced: 1060 us -> 357 us
  matrix products: 435 us -> 0 us
  local copies, waits for them, and re-layouts: 168 us -> 1.44 us
  other arithmetic: 131 us -> 3.15 us
  Pallas kernels: 0 us -> 81.8 us
  waiting for transfers between devices: 142 us -> 98.5 us
  blocking collectives: 167 us -> 154 us
    dot_general x10 -> x0, matrix products: 435 us -> none  [the longest x8 418 us: contract(): return jnp.einsum(form, left, table, preferred_element_type=jnp.float32)]
    another operation x8 -> x0, other arithmetic: 118 us -> none
    pallas_call x0 -> x7, Pallas kernels: none -> 81.8 us  [the longest x1 26.5 us: products(): pl.pallas_call(functools.partial(product_kernel, chunk), grid=(half // hb...]
    all_to_all x5 -> x0, local copies, waits for them, and re-layouts: 46.5 us -> none  [the longest x2 16.9 us: on_device(): lax.all_to_all(fields, 'row', split_axis=2, concat_axis=4, tiled=True)]
    all_to_all x2 -> x5, waiting for transfers between devices: 142 us -> 98.5 us  [exchange(): return lax.all_to_all(x, axis, split_axis=0, concat_axis=0, tiled=True)]
    unnamed x20 -> x8, local copies, waits for them, and re-layouts: 33.3 us -> 1.44 us
    another operation x1 -> x0, local copies, waits for them, and re-layouts: 22.3 us -> none
    pad x2 -> x0, local copies, waits for them, and re-layouts: 21.9 us -> none  [the longest x1 11.9 us: on_device(): jnp.pad(span_grid, ((0, 0), (0, 0), (0, 0), (0, stream_local // 2), (0, 0)))]
  transfers between devices with their start and end apart: 2 -> 5, of which waited for: 2 -> 5; matrix products, arithmetic and copies ran while one was open for 11% -> 0% of each run, Pallas kernels for 0% -> 14%
where the time goes in v1:
time: 360 us; the launch traced here: 357 us
  blocking collectives  154 us (43%)
  waiting for transfers between devices  98.5 us (27%)
  Pallas kernels  81.8 us (23%)
  starting transfers between devices  18.1 us (5%)
    all_to_all x5, blocking collectives, exchange(): return lax.all_to_all(x, axis, split_axis=0, concat_axis=0, tiled=True)  154 us
    all_to_all x5, waiting for transfers between devices, exchange(): return lax.all_to_all(x, axis, split_axis=0, concat_axis=0, tiled=True)  98.5 us
    pallas_call x1, Pallas kernels, products(): pl.pallas_call(functools.partial(product_kernel, chunk), grid=(half // hb...  26.5 us
    pallas_call x2, Pallas kernels, inverse_span(): pl.pallas_call(functools.partial(inverse_kernel, group, span_modes), grid...  24.9 us
    pallas_call x3, Pallas kernels, forward_span(): pl.pallas_call(functools.partial(forward_kernel, norm), grid=(row_count,)...  23.8 us
    all_to_all x5, starting transfers between devices, exchange(): return lax.all_to_all(x, axis, split_axis=0, concat_axis=0, tiled=True)  18.1 us
  transfers between devices with their start and end apart: 5, of which 5 were waited for; matrix products, arithmetic and copies ran while one was open for 0% of the time, Pallas kernels for 14%

profile of v1, /device:TPU:0, one launch (start us, length us, event | category | flops | bytes accessed | tf_op | source)
XLA Modules:
  0.0 356.9 jit_solution(13835106924295179096)
XLA Ops:
  0.0 6.6 %collocate.1 = (bf16[4,2,128,768]{3,2,1,0:T(8,128)(2,1)}, bf16[4,3,128,768]{3,2,1,0:T(8,128)(2,1)}) custom-call(f32[4,4]{1,0:T(4,128)} %values.1, f32[4,4]{1,0:T(4,128)} %slopes.1, s32[4]{0:T(128)} %offsets.1, f32[3,7,128,768]{3,2,1,0:T(8,128)} %coef.1), custom_call_target="tpu_custom_call" | custom-call | tf_op jit(solution)/shard_map/collocate/pallas_call | solution.py:68
  6.6 43.4 %all_to_all.50.x = bf16[4,2,128,768]{3,2,1,0:T(8,128)(2,1)} all-to-all(bf16[4,2,128,768]{3,2,1,0:T(8,128)(2,1)} %get-tuple-element.10), channel_id=1, replica_groups=mesh['row'=4,'col'=8] {'row'}, dimensions={0} | all-to-all | bytes 3145728 | tf_op jit(solution)/shard_map/all_to_all | solution.py:294
  50.0 3.6 %all-to-all-start.2 = ((bf16[4,3,128,768]{3,2,1,0:T(8,128)(2,1)}), bf16[4,3,128,768]{3,2,1,0:T(8,128)(2,1)S(1)}, u32[]{:S(2)}, u32[]{:S(2)}) async-start(bf16[4,3,128,768]{3,2,1,0:T(8,128)(2,1)} %get-tuple-element.11), calls=%async_computation.2 | async-start | bytes 4718592 | tf_op jit(solution)/shard_map/all_to_all | solution.py:294
  53.6 0.6 convert_multiply_fusion.stream_wave
  54.2 11.7 %inverse_span.2 = bf16[8,3,2,288,128]{4,3,2,1,0:T(8,128)(2,1)} custom-call(bf16[4,2,128,768]{3,2,1,0:T(8,128)(2,1)} %all_to_all.50.x, f32[1,128]{1,0:T(1,128)} %convert_multiply_fusion.stream_wave, bf16[768,768]{1,0:T(8,128)(2,1)} %constant.30.clone.split, bf16[1152,1536]{1,0:T(8,128)(2,1)} %constant.31.clone.cosine, bf16[1152,1536]{1,0:T(8,128)(2,1)} %constant.32.clone.sine), custom_call_target="tpu_custom_call" | custom-call | flops 5435817984 | bytes 10223616 | tf_op jit(solution)/shard_map/inverse_span/pallas_call | solution.py:153
  65.9 40.6 %all-to-all-done.2.x = bf16[4,3,128,768]{3,2,1,0:T(8,128)(2,1)S(1)} async-done(((bf16[4,3,128,768]{3,2,1,0:T(8,128)(2,1)}), bf16[4,3,128,768]{3,2,1,0:T(8,128)(2,1)S(1)}, u32[]{:S(2)}, u32[]{:S(2)}) %all-to-all-start.2) | async-done | bytes 2359328 | tf_op jit(solution)/shard_map/all_to_all | solution.py:294
  106.5 0.0 copy-start.2
  106.5 1.4 copy-done.2
  108.0 3.7 %all-to-all-start.1 = ((bf16[8,3,2,288,128]{4,3,2,1,0:T(8,128)(2,1)}), bf16[8,3,2,288,128]{4,3,2,1,0:T(8,128)(2,1)S(1)}, u32[]{:S(2)}, u32[]{:S(2)}) async-start(bf16[8,3,2,288,128]{4,3,2,1,0:T(8,128)(2,1)} %inverse_span.2), calls=%async_computation.1 | async-start | bytes 7077888 | tf_op jit(solution)/shard_map/all_to_all | solution.py:294
  111.7 13.2 %inverse_span.3 = bf16[8,3,2,288,128]{4,3,2,1,0:T(8,128)(2,1)} custom-call(bf16[4,3,128,768]{3,2,1,0:T(8,128)(2,1)} %copy-done.2, f32[1,128]{1,0:T(1,128)} %convert_multiply_fusion.stream_wave, bf16[768,768]{1,0:T(8,128)(2,1)} %constant.30.clone.split, bf16[1152,1536]{1,0:T(8,128)(2,1)} %constant.31.clone.cosine, bf16[1152,1536]{1,0:T(8,128)(2,1)} %constant.32.clone.sine), custom_call_target="tpu_custom_call" | custom-call | flops 5435817984 | bytes 11796480 | tf_op jit(solution)/shard_map/inverse_span/pallas_call | solution.py:153
  124.8 28.9 %all-to-all-done.1 = bf16[8,3,2,288,128]{4,3,2,1,0:T(8,128)(2,1)S(1)} async-done(((bf16[8,3,2,288,128]{4,3,2,1,0:T(8,128)(2,1)}), bf16[8,3,2,288,128]{4,3,2,1,0:T(8,128)(2,1)S(1)}, u32[]{:S(2)}, u32[]{:S(2)}) %all-to-all-start.1) | async-done | bytes 3538976 | tf_op jit(solution)/shard_map/all_to_all | solution.py:294
  153.8 0.0 copy-start.1
  153.8 46.5 %all_to_all.51 = bf16[8,3,2,288,128]{4,3,2,1,0:T(8,128)(2,1)} all-to-all(bf16[8,3,2,288,128]{4,3,2,1,0:T(8,128)(2,1)} %inverse_span.3), channel_id=1, replica_groups=mesh['row'=4,'col'=8] {'col'}, dimensions={0} | all-to-all | bytes 7077888 | tf_op jit(solution)/shard_map/all_to_all | solution.py:294
  200.3 0.0 copy-done.1
  200.3 26.5 %products.1 = (bf16[8,2,2,144,128]{4,3,2,1,0:T(8,128)(2,1)}, bf16[8,2,2,144,128]{4,3,2,1,0:T(8,128)(2,1)}, bf16[8,2,2,144,128]{4,3,2,1,0:T(8,128)(2,1)}) custom-call(bf16[8,3,2,2,144,128]{5,4,3,2,1,0:T(8,128)(2,1)} %bitcast.5, bf16[8,3,2,2,144,128]{5,4,3,2,1,0:T(8,128)(2,1)} %bitcast.6, bf16[1024,1536]{1,0:T(8,128)(2,1)} %constant.26.clone.wave_c, ...), custom_call_target="tpu_custom_call" | custom-call | flops 16307453952 | bytes 33816576 | tf_op jit(solution)/shard_map/products/pallas_call | solution.py:226
  226.8 0.0 copy-start.3
  226.8 21.1 %all_to_all.52.spectral = bf16[8,2,2,144,128]{4,3,2,1,0:T(8,128)(2,1)} all-to-all(bf16[8,2,2,144,128]{4,3,2,1,0:T(8,128)(2,1)} %get-tuple-element.12), channel_id=1, replica_groups=mesh['row'=4,'col'=8] {'col'}, dimensions={0} | all-to-all | bytes 2359296 | tf_op jit(solution)/shard_map/all_to_all | solution.py:294
  247.9 0.0 copy-done.3
  247.9 19.9 %all_to_all.53.spectral = bf16[8,2,2,144,128]{4,3,2,1,0:T(8,128)(2,1)} all-to-all(bf16[8,2,2,144,128]{4,3,2,1,0:T(8,128)(2,1)S(1)} %copy-done.3), channel_id=1, replica_groups=mesh['row'=4,'col'=8] {'col'}, dimensions={0} | all-to-all | bytes 2359296 | tf_op jit(solution)/shard_map/all_to_all | solution.py:294
  267.8 3.6 all-to-all-start.8
  271.4 7.9 %forward_span.3 = bf16[4,128,768]{2,1,0:T(8,128)(2,1)} custom-call(bf16[8,2,2,144,128]{4,3,2,1,0:T(8,128)(2,1)} %all_to_all.52.spectral, bf16[768,768]{1,0:T(8,128)(2,1)} %constant.30.clone.split, bf16[1536,1152]{1,0:T(8,128)(2,1)} %constant.33.clone.cosine, bf16[1536,1152]{1,0:T(8,128)(2,1)} %constant.34.clone.sine), custom_call_target="tpu_custom_call" | custom-call | flops 1811939328 | bytes 9437184 | tf_op jit(solution)/shard_map/forward_span/pallas_call | solution.py:276
  279.3 8.8 %all-to-all-done.8.spectral = bf16[8,2,2,144,128]{4,3,2,1,0:T(8,128)(2,1)S(1)} async-done(((bf16[8,2,2,144,128]{4,3,2,1,0:T(8,128)(2,1)}), bf16[8,2,2,144,128]{4,3,2,1,0:T(8,128)(2,1)S(1)}, u32[]{:S(2)}, u32[]{:S(2)}) %all-to-all-start.8) | async-done | bytes 1179680 | tf_op jit(solution)/shard_map/all_to_all | solution.py:294
  288.1 0.0 copy-start
  288.1 3.7 %all-to-all-start.5 = ((bf16[4,128,768]{2,1,0:T(8,128)(2,1)}), bf16[4,128,768]{2,1,0:T(8,128)(2,1)S(1)}, u32[]{:S(2)}, u32[]{:S(2)}) async-start(bf16[4,128,768]{2,1,0:T(8,128)(2,1)} %forward_span.3), calls=%async_computation.5 | async-start | bytes 1572864 | tf_op jit(solution)/shard_map/all_to_all | solution.py:294
  291.8 7.9 %forward_span.4 = bf16[4,128,768]{2,1,0:T(8,128)(2,1)} custom-call(bf16[8,2,2,144,128]{4,3,2,1,0:T(8,128)(2,1)} %all_to_all.53.spectral, bf16[768,768]{1,0:T(8,128)(2,1)} %constant.30.clone.split, bf16[1536,1152]{1,0:T(8,128)(2,1)} %constant.33.clone.cosine, bf16[1536,1152]{1,0:T(8,128)(2,1)} %constant.34.clone.sine), custom_call_target="tpu_custom_call" | custom-call | flops 1811939328 | bytes 9437184 | tf_op jit(solution)/shard_map/forward_span/pallas_call | solution.py:276
  299.8 0.0 copy-done
  299.8 9.4 %all-to-all-done.5 = bf16[4,128,768]{2,1,0:T(8,128)(2,1)S(1)} async-done(((bf16[4,128,768]{2,1,0:T(8,128)(2,1)}), bf16[4,128,768]{2,1,0:T(8,128)(2,1)S(1)}, u32[]{:S(2)}, u32[]{:S(2)}) %all-to-all-start.5) | async-done | bytes 786464 | tf_op jit(solution)/shard_map/all_to_all | solution.py:294
  309.1 3.5 all-to-all-start.7
  312.6 7.9 %forward_span.5 = bf16[4,128,768]{2,1,0:T(8,128)(2,1)} custom-call(bf16[8,2,2,144,128]{4,3,2,1,0:T(8,128)(2,1)} %copy-done, bf16[768,768]{1,0:T(8,128)(2,1)} %constant.30.clone.split, bf16[1536,1152]{1,0:T(8,128)(2,1)} %constant.33.clone.cosine, bf16[1536,1152]{1,0:T(8,128)(2,1)} %constant.34.clone.sine), custom_call_target="tpu_custom_call" | custom-call | flops 1811939328 | bytes 9437184 | tf_op jit(solution)/shard_map/forward_span/pallas_call | solution.py:276
  320.6 10.7 %all-to-all-done.7 = bf16[4,128,768]{2,1,0:T(8,128)(2,1)S(1)} async-done(((bf16[4,128,768]{2,1,0:T(8,128)(2,1)}), bf16[4,128,768]{2,1,0:T(8,128)(2,1)S(1)}, u32[]{:S(2)}, u32[]{:S(2)}) %all-to-all-start.7) | async-done | bytes 786464 | tf_op jit(solution)/shard_map/all_to_all | solution.py:294
  331.3 23.1 %all_to_all.54 = bf16[4,128,768]{2,1,0:T(8,128)(2,1)S(1)} all-to-all(bf16[4,128,768]{2,1,0:T(8,128)(2,1)} %forward_span.5), channel_id=1, replica_groups=mesh['row'=4,'col'=8] {'row'}, dimensions={0} | all-to-all | bytes 1572864 | tf_op jit(solution)/shard_map/all_to_all | solution.py:294
  354.4 2.6 maximum_convert_fusion
Async XLA Ops:
  50.0 56.6 %all-to-all-start.2 = ((bf16[4,3,128,768]{3,2,1,0:T(8,128)(2,1)}), bf16[4,3,128,768]{3,2,1,0:T(8,128)(2,1)S(1)}, u32[]{:S(2)}, u32[]{:S(2)}) async-start(bf16[4,3,128,768]{3,2,1,0:T(8,128)(2,1)} %get-tuple-element.11), calls=%async_computation.2 | async-start | bytes 4718592 | tf_op jit(solution)/shard_map/all_to_all | solution.py:294
  106.5 1.4 copy-start.2
  108.0 45.8 %all-to-all-start.1 = ((bf16[8,3,2,288,128]{4,3,2,1,0:T(8,128)(2,1)}), bf16[8,3,2,288,128]{4,3,2,1,0:T(8,128)(2,1)S(1)}, u32[]{:S(2)}, u32[]{:S(2)}) async-start(bf16[8,3,2,288,128]{4,3,2,1,0:T(8,128)(2,1)} %inverse_span.2), calls=%async_computation.1 | async-start | bytes 7077888 | tf_op jit(solution)/shard_map/all_to_all | solution.py:294
  153.8 46.5 %copy-start.1 = (bf16[8,3,2,288,128]{4,3,2,1,0:T(8,128)(2,1)}, bf16[8,3,2,288,128]{4,3,2,1,0:T(8,128)(2,1)S(1)}, u32[]{:S(2)}) copy-start(bf16[8,3,2,288,128]{4,3,2,1,0:T(8,128)(2,1)S(1)} %all-to-all-done.1) | copy-start | bytes 10616836
  226.8 21.2 %copy-start.3 = (bf16[8,2,2,144,128]{4,3,2,1,0:T(8,128)(2,1)S(1)}, bf16[8,2,2,144,128]{4,3,2,1,0:T(8,128)(2,1)}, u32[]{:S(2)}) copy-start(bf16[8,2,2,144,128]{4,3,2,1,0:T(8,128)(2,1)} %get-tuple-element.13) | copy-start | bytes 3538948
  267.8 20.3 %all-to-all-start.8 = ((bf16[8,2,2,144,128]{4,3,2,1,0:T(8,128)(2,1)}), bf16[8,2,2,144,128]{4,3,2,1,0:T(8,128)(2,1)S(1)}, u32[]{:S(2)}, u32[]{:S(2)}) async-start(bf16[8,2,2,144,128]{4,3,2,1,0:T(8,128)(2,1)} %get-tuple-element.14), calls=%async_computation.8 | async-start | bytes 2359296 | tf_op jit(solution)/shard_map/all_to_all | solution.py:294
  288.1 11.6 %copy-start = (bf16[8,2,2,144,128]{4,3,2,1,0:T(8,128)(2,1)}, bf16[8,2,2,144,128]{4,3,2,1,0:T(8,128)(2,1)S(1)}, u32[]{:S(2)}) copy-start(bf16[8,2,2,144,128]{4,3,2,1,0:T(8,128)(2,1)S(1)} %all-to-all-done.8.spectral) | copy-start | bytes 3538948
  288.1 21.0 %all-to-all-start.5 = ((bf16[4,128,768]{2,1,0:T(8,128)(2,1)}), bf16[4,128,768]{2,1,0:T(8,128)(2,1)S(1)}, u32[]{:S(2)}, u32[]{:S(2)}) async-start(bf16[4,128,768]{2,1,0:T(8,128)(2,1)} %forward_span.3), calls=%async_computation.5 | async-start | bytes 1572864 | tf_op jit(solution)/shard_map/all_to_all | solution.py:294
  309.1 22.2 %all-to-all-start.7 = ((bf16[4,128,768]{2,1,0:T(8,128)(2,1)}), bf16[4,128,768]{2,1,0:T(8,128)(2,1)S(1)}, u32[]{:S(2)}, u32[]{:S(2)}) async-start(bf16[4,128,768]{2,1,0:T(8,128)(2,1)} %forward_span.4), calls=%async_computation.7 | async-start | bytes 1572864 | tf_op jit(solution)/shard_map/all_to_all | solution.py:294

commit v2 on v1

--- a/solution.py
+++ b/solution.py
@@ -245,49 +245,123 @@
     )(ga, gb, *tables)
 
 
-def forward_kernel(norm, spectral, split, cosine, sine, out, plus, minus):
-    cols, _, _, block, lanes = spectral.shape
-
-    @pl.when(pl.program_id(0) == 0)
-    def _():
+def finish_kernel(norm, t0, t1, t2, split, cosine, sine, out, got, plus, minus, made, col_send, col_recv, row_send, row_recv, own):
+    _, cols, _, _, block, lanes = got.shape
+    _, rows, _, width = made.shape
+    half = width // 2
+    col, row = lax.axis_index("col"), lax.axis_index("row")
+    mesh_ids = pl.DeviceIdType.MESH
+    col_peers = [lax.rem(col + k, cols) for k in range(1, cols)]
+    row_peers = [lax.rem(row + k, rows) for k in range(1, rows)]
+
+    barrier = pltpu.get_barrier_semaphore()
+    for peer in col_peers:
+        pl.semaphore_signal(barrier, inc=1, device_id={"col": peer}, device_id_type=mesh_ids)
+    for peer in row_peers:
+        pl.semaphore_signal(barrier, inc=1, device_id={"row": peer}, device_id_type=mesh_ids)
+    pl.semaphore_wait(barrier, cols + rows - 2)
+
+    terms = (t0, t1, t2)
+
+    def start_cols(c):
+        copies = [pltpu.make_async_copy(terms[c].at[col], got.at[c, col], own.at[0, c])]
+        for k, peer in enumerate(col_peers):
+            copies.append(
+                pltpu.make_async_remote_copy(
+                    src_ref=terms[c].at[peer],
+                    dst_ref=got.at[c, col],
+                    send_sem=col_send.at[c, k],
+                    recv_sem=col_recv.at[c, k],
+                    device_id={"col": peer},
+                    device_id_type=mesh_ids,
+                )
+            )
+        for copy in copies:
+            copy.start()
+        return copies
+
+    def start_rows(c):
+        copies = []
+        for k, peer in enumerate(row_peers):
+            copies.append(
+                pltpu.make_async_remote_copy(
+                    src_ref=made.at[c, peer],
+                    dst_ref=out.at[c, row],
+                    send_sem=row_send.at[c, k],
+                    recv_sem=row_recv.at[c, k],
+                    device_id={"row": peer},
+                    device_id_type=mesh_ids,
+                )
+            )
+        copies.append(pltpu.make_async_copy(made.at[c, row], out.at[c, row], own.at[1, c]))
+        for copy in copies:
+            copy.start()
+        return copies
+
+    sent = []
+    moving = start_cols(0)
+    for c in range(3):
+        for copy in moving:
+            copy.wait()
+        if c < 2:
+            moving = start_cols(c + 1)
         for d in range(cols):
             here = slice(d * block, (d + 1) * block)
             for p in range(2):
                 at = slice(p * lanes, (p + 1) * lanes)
-                plus[here, at] = spectral[d, p, 0]
-                minus[here, at] = spectral[d, p, 1]
-
-    by_cosine = dot(cosine[...], plus[...])
-    by_sine = dot(sine[...], minus[...])
-    re = (by_cosine[:, :lanes] + by_sine[:, lanes:]) * norm
-    im = (by_cosine[:, lanes:] - by_sine[:, :lanes]) * norm
-    parts = jnp.concatenate([re, im], axis=0).astype(BF)
-    out[0] = lax.dot_general(
-        parts, split[...], (((0,), (0,)), ((), ())), preferred_element_type=F32
-    ).astype(BF)
-
-
-def forward_span(spectral, split, cosine, sine, norm, row_count):
-    cols, _, _, block, lanes = spectral.shape
+                plus[here, at] = got[c, d, p, 0]
+                minus[here, at] = got[c, d, p, 1]
+
+        def body(r, carry, c=c):
+            at = pl.ds(pl.multiple_of(r * half, 16), half)
+            by_cosine = dot(cosine[at, :], plus[...])
+            by_sine = dot(sine[at, :], minus[...])
+            re = (by_cosine[:, :lanes] + by_sine[:, lanes:]) * norm
+            im = (by_cosine[:, lanes:] - by_sine[:, :lanes]) * norm
+            parts = jnp.concatenate([re, im], axis=0).astype(BF)
+            made[c, r] = lax.dot_general(
+                parts, split[...], (((0,), (0,)), ((), ())), preferred_element_type=F32
+            ).astype(BF)
+            return carry
+
+        lax.fori_loop(0, rows, body, 0)
+        sent += start_rows(c)
+    for copy in sent:
+        copy.wait()
+
+
+def finish(terms, split, cosine, sine, norm, row_count):
+    cols, _, _, block, lanes = terms[0].shape
     span_modes, half_points = cosine.shape
     width = 2 * span_modes // row_count
-    whole = lambda a: pl.BlockSpec(a.shape, lambda i: (0,) * a.ndim)
-    table = pl.BlockSpec((width // 2, half_points), lambda i: (i, 0))
+    hbm = pl.BlockSpec(memory_space=pl.ANY)
+    vmem = pl.BlockSpec(memory_space=pltpu.VMEM)
     return pl.pallas_call(
-        functools.partial(forward_kernel, norm),
-        grid=(row_count,),
-        in_specs=[whole(spectral), whole(split), table, table],
-        out_specs=pl.BlockSpec((1, lanes, width), lambda i: (i, 0, 0)),
-        out_shape=jax.ShapeDtypeStruct((row_count, lanes, width), BF),
-        scratch_shapes=[pltpu.VMEM((half_points, 2 * lanes), BF)] * 2,
-        compiler_params=pltpu.CompilerParams(vmem_limit_bytes=VMEM_LIMIT),
+        functools.partial(finish_kernel, norm),
+        in_specs=[hbm] * 3 + [vmem] * 3,
+        out_specs=hbm,
+        out_shape=jax.ShapeDtypeStruct((3, row_count, lanes, width), BF),
+        scratch_shapes=[
+            pltpu.VMEM((3,) + terms[0].shape, BF),
+            pltpu.VMEM((half_points, 2 * lanes), BF),
+            pltpu.VMEM((half_points, 2 * lanes), BF),
+            pltpu.VMEM((3, row_count, lanes, width), BF),
+            pltpu.SemaphoreType.DMA((3, cols - 1)),
+            pltpu.SemaphoreType.DMA((3, cols - 1)),
+            pltpu.SemaphoreType.DMA((3, row_count - 1)),
+            pltpu.SemaphoreType.DMA((3, row_count - 1)),
+            pltpu.SemaphoreType.DMA((2, 3)),
+        ],
+        compiler_params=pltpu.CompilerParams(
+            collective_id=0, has_side_effects=True, vmem_limit_bytes=VMEM_LIMIT
+        ),
         cost_estimate=pl.CostEstimate(
-            flops=2 * 4 * lanes * span_modes * half_points,
-            bytes_accessed=4 * half_points * span_modes + 4 * spectral.size,
+            flops=2 * 12 * lanes * span_modes * half_points,
+            bytes_accessed=4 * half_points * span_modes + 24 * terms[0].size,
             transcendentals=0,
         ),
-        name="forward_span",
-    )(spectral, split, cosine, sine)
+        name="finish",
+    )(*terms, split, cosine, sine)
 
 
 def exchange(x, axis):
@@ -324,11 +398,7 @@
         grids.append(exchange(grid, "col"))
     half = span_points // 2 // col_count
     terms = products(*grids, stream, 48 if half % 48 == 0 else half, 512)
-    results = []
-    for term in terms:
-        spectrum = forward_span(exchange(term, "col"), split, *back, norm, row_count)
-        results.append(exchange(spectrum, "row"))
-    return jnp.stack(results).astype(F32)
+    return finish(terms, split, *back, norm, row_count).astype(F32)
 
 
 def solution(mesh):

time: 360 us -> 306 us (0.85)
  blocking collectives: 154 us -> 89.9 us
  Pallas kernels: 81.8 us -> 130 us
  waiting for transfers between devices: 98.5 us -> 69.6 us
  starting transfers between devices: 18.1 us -> 7.35 us
    all_to_all x5 -> x2, blocking collectives: 154 us -> 89.9 us  [exchange(): return lax.all_to_all(x, axis, split_axis=0, concat_axis=0, tiled=True)]
    pallas_call x3 -> x1, Pallas kernels: 23.8 us -> 72 us  [finish(): pl.pallas_call(functools.partial(finish_kernel, norm), in_specs=[hbm] * 3...]
    all_to_all x5 -> x2, waiting for transfers between devices: 98.5 us -> 69.6 us  [exchange(): return lax.all_to_all(x, axis, split_axis=0, concat_axis=0, tiled=True)]
    all_to_all x5 -> x2, starting transfers between devices: 18.1 us -> 7.35 us  [exchange(): return lax.all_to_all(x, axis, split_axis=0, concat_axis=0, tiled=True)]
  transfers between devices with their start and end apart: 5 -> 2, of which waited for: 5 -> 2; matrix products, arithmetic and copies ran while one was open for 0% -> 0% of each run, Pallas kernels for 14% -> 8%
where the time goes in v2:
time: 306 us; the launch traced here: 303 us
  Pallas kernels  130 us (42%)
  blocking collectives  89.9 us (29%)
  waiting for transfers between devices  69.6 us (23%)
  starting transfers between devices  7.35 us (2%)
  other arithmetic  4.83 us (2%)
    all_to_all x2, blocking collectives, exchange(): return lax.all_to_all(x, axis, split_axis=0, concat_axis=0, tiled=True)  89.9 us
    pallas_call x1, Pallas kernels, finish(): pl.pallas_call(functools.partial(finish_kernel, norm), in_specs=[hbm] * 3...  72 us
    all_to_all x2, waiting for transfers between devices, exchange(): return lax.all_to_all(x, axis, split_axis=0, concat_axis=0, tiled=True)  69.6 us
    pallas_call x1, Pallas kernels, products(): pl.pallas_call(functools.partial(product_kernel, chunk), grid=(half // hb...  26.5 us
    pallas_call x2, Pallas kernels, inverse_span(): pl.pallas_call(functools.partial(inverse_kernel, group, span_modes), grid...  24.9 us
    all_to_all x2, starting transfers between devices, exchange(): return lax.all_to_all(x, axis, split_axis=0, concat_axis=0, tiled=True)  7.35 us
    pallas_call x1, Pallas kernels, collocate(): pl.pallas_call(collocate_kernel, grid=(stream_local // rows,), in_specs=[...  6.52 us
  transfers between devices with their start and end apart: 2, of which 2 were waited for; matrix products, arithmetic and copies ran while one was open for 0% of the time, Pallas kernels for 8%

profile of v2, /device:TPU:0, one launch (start us, length us, event | category | flops | bytes accessed | tf_op | source)
XLA Modules:
  0.0 303.1 jit_solution(15720521813217781134)
XLA Ops:
  0.0 6.5 %collocate.1 = (bf16[4,2,128,768]{3,2,1,0:T(8,128)(2,1)}, bf16[4,3,128,768]{3,2,1,0:T(8,128)(2,1)}) custom-call(f32[4,4]{1,0:T(4,128)} %values.1, f32[4,4]{1,0:T(4,128)} %slopes.1, s32[4]{0:T(128)} %offsets.1, f32[3,7,128,768]{3,2,1,0:T(8,128)} %coef.1), custom_call_target="tpu_custom_call" | custom-call | tf_op jit(solution)/shard_map/collocate/pallas_call | solution.py:68
  6.5 43.4 %all_to_all.20.x = bf16[4,2,128,768]{3,2,1,0:T(8,128)(2,1)} all-to-all(bf16[4,2,128,768]{3,2,1,0:T(8,128)(2,1)} %get-tuple-element.10), channel_id=1, replica_groups=mesh['row'=4,'col'=8] {'row'}, dimensions={0} | all-to-all | bytes 3145728 | tf_op jit(solution)/shard_map/all_to_all | solution.py:368
  49.9 3.6 %all-to-all-start.2 = ((bf16[4,3,128,768]{3,2,1,0:T(8,128)(2,1)}), bf16[4,3,128,768]{3,2,1,0:T(8,128)(2,1)S(1)}, u32[]{:S(2)}, u32[]{:S(2)}) async-start(bf16[4,3,128,768]{3,2,1,0:T(8,128)(2,1)} %get-tuple-element.11), calls=%async_computation.2 | async-start | bytes 4718592 | tf_op jit(solution)/shard_map/all_to_all | solution.py:368
  53.5 0.5 convert_multiply_fusion.stream_wave
  54.1 11.7 %inverse_span.2 = bf16[8,3,2,288,128]{4,3,2,1,0:T(8,128)(2,1)} custom-call(bf16[4,2,128,768]{3,2,1,0:T(8,128)(2,1)} %all_to_all.20.x, f32[1,128]{1,0:T(1,128)} %convert_multiply_fusion.stream_wave, bf16[768,768]{1,0:T(8,128)(2,1)} %constant.30.clone.split, bf16[1152,1536]{1,0:T(8,128)(2,1)} %constant.31.clone.cosine, bf16[1152,1536]{1,0:T(8,128)(2,1)} %constant.32.clone.sine), custom_call_target="tpu_custom_call" | custom-call | flops 5435817984 | bytes 10223616 | tf_op jit(solution)/shard_map/inverse_span/pallas_call | solution.py:153
  65.8 40.7 %all-to-all-done.2.x = bf16[4,3,128,768]{3,2,1,0:T(8,128)(2,1)S(1)} async-done(((bf16[4,3,128,768]{3,2,1,0:T(8,128)(2,1)}), bf16[4,3,128,768]{3,2,1,0:T(8,128)(2,1)S(1)}, u32[]{:S(2)}, u32[]{:S(2)}) %all-to-all-start.2) | async-done | bytes 2359328 | tf_op jit(solution)/shard_map/all_to_all | solution.py:368
  106.5 0.0 copy-start.1
  106.5 1.4 copy-done.1
  107.9 3.7 %all-to-all-start.1 = ((bf16[8,3,2,288,128]{4,3,2,1,0:T(8,128)(2,1)}), bf16[8,3,2,288,128]{4,3,2,1,0:T(8,128)(2,1)S(1)}, u32[]{:S(2)}, u32[]{:S(2)}) async-start(bf16[8,3,2,288,128]{4,3,2,1,0:T(8,128)(2,1)} %inverse_span.2), calls=%async_computation.1 | async-start | bytes 7077888 | tf_op jit(solution)/shard_map/all_to_all | solution.py:368
  111.6 13.1 %inverse_span.3 = bf16[8,3,2,288,128]{4,3,2,1,0:T(8,128)(2,1)} custom-call(bf16[4,3,128,768]{3,2,1,0:T(8,128)(2,1)} %copy-done.1, f32[1,128]{1,0:T(1,128)} %convert_multiply_fusion.stream_wave, bf16[768,768]{1,0:T(8,128)(2,1)} %constant.30.clone.split, bf16[1152,1536]{1,0:T(8,128)(2,1)} %constant.31.clone.cosine, bf16[1152,1536]{1,0:T(8,128)(2,1)} %constant.32.clone.sine), custom_call_target="tpu_custom_call" | custom-call | flops 5435817984 | bytes 11796480 | tf_op jit(solution)/shard_map/inverse_span/pallas_call | solution.py:153
  124.8 28.9 %all-to-all-done.1 = bf16[8,3,2,288,128]{4,3,2,1,0:T(8,128)(2,1)S(1)} async-done(((bf16[8,3,2,288,128]{4,3,2,1,0:T(8,128)(2,1)}), bf16[8,3,2,288,128]{4,3,2,1,0:T(8,128)(2,1)S(1)}, u32[]{:S(2)}, u32[]{:S(2)}) %all-to-all-start.1) | async-done | bytes 3538976 | tf_op jit(solution)/shard_map/all_to_all | solution.py:368
  153.7 0.0 copy-start
  153.7 46.5 %all_to_all.21 = bf16[8,3,2,288,128]{4,3,2,1,0:T(8,128)(2,1)} all-to-all(bf16[8,3,2,288,128]{4,3,2,1,0:T(8,128)(2,1)} %inverse_span.3), channel_id=1, replica_groups=mesh['row'=4,'col'=8] {'col'}, dimensions={0} | all-to-all | bytes 7077888 | tf_op jit(solution)/shard_map/all_to_all | solution.py:368
  200.2 0.0 copy-done
  200.2 26.5 %products.1 = (bf16[8,2,2,144,128]{4,3,2,1,0:T(8,128)(2,1)}, bf16[8,2,2,144,128]{4,3,2,1,0:T(8,128)(2,1)}, bf16[8,2,2,144,128]{4,3,2,1,0:T(8,128)(2,1)}) custom-call(bf16[8,3,2,2,144,128]{5,4,3,2,1,0:T(8,128)(2,1)} %bitcast.2, bf16[8,3,2,2,144,128]{5,4,3,2,1,0:T(8,128)(2,1)} %bitcast.3, bf16[1024,1536]{1,0:T(8,128)(2,1)} %constant.26.clone.wave_c, ...), custom_call_target="tpu_custom_call" | custom-call | flops 16307453952 | bytes 33816576 | tf_op jit(solution)/shard_map/products/pallas_call | solution.py:226
  226.7 72.0 %finish.1 = bf16[3,4,128,768]{3,2,1,0:T(8,128)(2,1)} custom-call(bf16[8,2,2,144,128]{4,3,2,1,0:T(8,128)(2,1)} %get-tuple-element.12.t0, bf16[8,2,2,144,128]{4,3,2,1,0:T(8,128)(2,1)} %get-tuple-element.13.t1, bf16[8,2,2,144,128]{4,3,2,1,0:T(8,128)(2,1)} %get-tuple-element.14.t2, bf16[768,768]{1,0:T(8,128)(2,1)} %constant.30.clone.split, ...), custom_call_target="tpu_custom_call" | custom-call | flops 5435817984 | bytes 21233664 | tf_op jit(solution)/shard_map/finish/pallas_call | solution.py:339
  298.8 4.3 %convert_element_type.14 = f32[3,4,128,768]{3,2,1,0:T(8,128)} convert(bf16[3,4,128,768]{3,2,1,0:T(8,128)(2,1)} %finish.1) | non-fusion elementwise | flops 1179648 | bytes 7077888 | tf_op jit(solution)/shard_map/convert_element_type | solution.py:401
Async XLA Ops:
  49.9 56.6 %all-to-all-start.2 = ((bf16[4,3,128,768]{3,2,1,0:T(8,128)(2,1)}), bf16[4,3,128,768]{3,2,1,0:T(8,128)(2,1)S(1)}, u32[]{:S(2)}, u32[]{:S(2)}) async-start(bf16[4,3,128,768]{3,2,1,0:T(8,128)(2,1)} %get-tuple-element.11), calls=%async_computation.2 | async-start | bytes 4718592 | tf_op jit(solution)/shard_map/all_to_all | solution.py:368
  106.5 1.4 copy-start.1
  107.9 45.8 %all-to-all-start.1 = ((bf16[8,3,2,288,128]{4,3,2,1,0:T(8,128)(2,1)}), bf16[8,3,2,288,128]{4,3,2,1,0:T(8,128)(2,1)S(1)}, u32[]{:S(2)}, u32[]{:S(2)}) async-start(bf16[8,3,2,288,128]{4,3,2,1,0:T(8,128)(2,1)} %inverse_span.2), calls=%async_computation.1 | async-start | bytes 7077888 | tf_op jit(solution)/shard_map/all_to_all | solution.py:368
  153.7 46.5 %copy-start = (bf16[8,3,2,288,128]{4,3,2,1,0:T(8,128)(2,1)}, bf16[8,3,2,288,128]{4,3,2,1,0:T(8,128)(2,1)S(1)}, u32[]{:S(2)}) copy-start(bf16[8,3,2,288,128]{4,3,2,1,0:T(8,128)(2,1)S(1)} %all-to-all-done.1) | copy-start | bytes 10616836

commit v3 on v2

--- a/solution.py
+++ b/solution.py
@@ -82,91 +82,172 @@
     )(values, slopes, offsets, coefficients)
 
 
-def inverse_kernel(group, span_modes, x, stream_wave, split, cosine, sine, out, modes):
+def lift_modes(group, span_modes, x, stream_wave, split, modes):
     rows, sent, stream_local, width = x.shape
     half = width // 2
-
-    @pl.when(pl.program_id(0) == 0)
-    def _():
-        wave_x = stream_wave[...]
-
-        def body(r, carry):
-            flat = x[r].reshape(sent * stream_local, width)
-            parts = lax.dot_general(
-                split[...], flat, (((1,), (1,)), ((), ())), preferred_element_type=F32
+    wave_x = stream_wave[...]
+
+    def body(r, carry):
+        flat = x[r].reshape(sent * stream_local, width)
+        parts = lax.dot_general(
+            split[...], flat, (((1,), (1,)), ((), ())), preferred_element_type=F32
+        )
+        field = lambda k: (
+            parts[:half, k * stream_local : (k + 1) * stream_local],
+            parts[half:, k * stream_local : (k + 1) * stream_local],
+        )
+        mode = r * half + lax.broadcasted_iota(jnp.int32, (half, stream_local), 0)
+        signed = jnp.where(mode < span_modes // 2, mode, mode - span_modes)
+        wave_z = signed.astype(F32) * span_unit
+        if group == 0:
+            (ur, ui), (wr, wi) = field(0), field(1)
+            fields = [
+                (ur, ui),
+                (wr, wi),
+                (-(wave_x * wi - wave_z * ui), wave_x * wr - wave_z * ur),
+            ]
+        else:
+            (vr, vi), (sur, sui), (swr, swi) = field(0), field(1), field(2)
+            fields = [
+                (vr, vi),
+                (-wave_z * vi - swr, wave_z * vr - swi),
+                (sur + wave_x * vi, sui - wave_x * vr),
+            ]
+        here = pl.ds(pl.multiple_of(r * half, 16), half)
+        for f in range(3):
+            for p in range(2):
+                at = (p * 3 + f) * stream_local
+                modes[here, at : at + stream_local] = fields[f][p].astype(BF)
+        return carry
+
+    lax.fori_loop(0, rows, body, 0)
+
+
+def start_kernel(
+    a, b, stream_wave, split, cosine, sine, ga, gb,
+    xa, xb, modes, made, row_send, row_recv, col_send, col_recv, own,
+):
+    rows, _, stream_local, _ = xa.shape
+    cols = ga.shape[0]
+    pairs = cols // 2
+    block = ga.shape[3] // 2
+    span_modes = cosine.shape[1]
+    col, row = lax.axis_index("col"), lax.axis_index("row")
+    pair, core = col // 2, lax.rem(col, 2)
+    mesh_ids = pl.DeviceIdType.MESH
+    row_peers = [lax.rem(row + k, rows) for k in range(1, rows)]
+
+    barrier = pltpu.get_barrier_semaphore()
+    for k in range(1, cols):
+        peer = lax.rem(col + k, cols)
+        pl.semaphore_signal(barrier, inc=1, device_id={"col": peer}, device_id_type=mesh_ids)
+    for peer in row_peers:
+        pl.semaphore_signal(barrier, inc=1, device_id={"row": peer}, device_id_type=mesh_ids)
+    pl.semaphore_wait(barrier, cols + rows - 2)
+
+    def start_rows(g):
+        source, target = ((a, xa), (b, xb))[g]
+        copies = [pltpu.make_async_copy(source.at[row], target.at[row], own.at[0, g])]
+        for k, peer in enumerate(row_peers):
+            copies.append(
+                pltpu.make_async_remote_copy(
+                    src_ref=source.at[peer],
+                    dst_ref=target.at[row],
+                    send_sem=row_send.at[g, k],
+                    recv_sem=row_recv.at[g, k],
+                    device_id={"row": peer},
+                    device_id_type=mesh_ids,
+                )
             )
-            field = lambda k: (
-                parts[:half, k * stream_local : (k + 1) * stream_local],
-                parts[half:, k * stream_local : (k + 1) * stream_local],
+        for copy in copies:
+            copy.start()
+        return copies
+
+    def start_col(g, turn, other):
+        to_pair = lax.rem(pair + turn, pairs)
+        peer = to_pair * 2 + lax.rem(core + other, 2)
+        grid = (ga, gb)[g]
+        if turn == 0 and other == 0:
+            copy = pltpu.make_async_copy(made.at[g, col], grid.at[col], own.at[1, g])
+        else:
+            copy = pltpu.make_async_remote_copy(
+                src_ref=made.at[g, peer],
+                dst_ref=grid.at[col],
+                send_sem=col_send.at[g, turn, other],
+                recv_sem=col_recv.at[g, turn, other],
+                device_id={"col": peer},
+                device_id_type=mesh_ids,
             )
-            mode = r * half + lax.broadcasted_iota(jnp.int32, (half, stream_local), 0)
-            signed = jnp.where(mode < span_modes // 2, mode, mode - span_modes)
-            wave_z = signed.astype(F32) * span_unit
-            if group == 0:
-                (ur, ui), (wr, wi) = field(0), field(1)
-                fields = [
-                    (ur, ui),
-                    (wr, wi),
-                    (-(wave_x * wi - wave_z * ui), wave_x * wr - wave_z * ur),
-                ]
-            else:
-                (vr, vi), (sur, sui), (swr, swi) = field(0), field(1), field(2)
-                fields = [
-                    (vr, vi),
-                    (-wave_z * vi - swr, wave_z * vr - swi),
-                    (sur + wave_x * vi, sui - wave_x * vr),
-                ]
-            here = pl.ds(pl.multiple_of(r * half, 16), half)
-            for f in range(3):
-                for p in range(2):
-                    at = (p * 3 + f) * stream_local
-                    modes[here, at : at + stream_local] = fields[f][p].astype(BF)
-            return carry
-
-        lax.fori_loop(0, rows, body, 0)
-
-    by_cosine = dot(cosine[...], modes[...])
-    by_sine = dot(sine[...], modes[...])
+        copy.start()
+        return copy
+
     part = 3 * stream_local
-    pairs = [
-        (by_cosine[:, :part], -by_sine[:, part:]),
-        (by_cosine[:, part:], by_sine[:, :part]),
-    ]
-    block = out.shape[3] // 2
-    for p, (even, odd) in enumerate(pairs):
-        plus = (even + odd).astype(BF)
-        minus = (even - odd).astype(BF)
-        for d in range(out.shape[0]):
-            for f in range(3):
-                lanes = slice(f * stream_local, (f + 1) * stream_local)
-                out[d, f, p, :block] = plus[d * block : (d + 1) * block, lanes]
-                out[d, f, p, block:] = minus[d * block : (d + 1) * block, lanes]
-
-
-def inverse_span(group, x, stream_wave, split, cosine, sine, col_count):
-    rows, sent, stream_local, width = x.shape
+    sent = []
+    moving = start_rows(0)
+    for g in range(2):
+        for copy in moving:
+            copy.wait()
+        if g == 0:
+            moving = start_rows(1)
+        lift_modes(g, span_modes, (xa, xb)[g], stream_wave, split, modes)
+        for step in range(pairs):
+            turn = (step + 1) % pairs
+            to_pair = lax.rem(pair + turn, pairs)
+            at = pl.ds(pl.multiple_of(to_pair * 2 * block, 16), 2 * block)
+            by_cosine = dot(cosine[at, :], modes[...])
+            by_sine = dot(sine[at, :], modes[...])
+            sums = [
+                (by_cosine[:, :part], -by_sine[:, part:]),
+                (by_cosine[:, part:], by_sine[:, :part]),
+            ]
+            for p, (even, odd) in enumerate(sums):
+                plus = (even + odd).astype(BF)
+                minus = (even - odd).astype(BF)
+                for d in range(2):
+                    for f in range(3):
+                        lanes = slice(f * stream_local, (f + 1) * stream_local)
+                        made[g, to_pair * 2 + d, f, p, :block] = plus[d * block : (d + 1) * block, lanes]
+                        made[g, to_pair * 2 + d, f, p, block:] = minus[d * block : (d + 1) * block, lanes]
+            for other in range(2):
+                sent.append(start_col(g, turn, other))
+    for copy in sent:
+        copy.wait()
+
+
+def start(sent, stream_wave, split, cosine, sine, col_count):
+    a, b = sent
+    rows, _, stream_local, _ = a.shape
     half_points, span_modes = cosine.shape
     block = half_points // col_count
-    step = 2
-    whole = lambda a: pl.BlockSpec(a.shape, lambda i: (0,) * a.ndim)
-    table = pl.BlockSpec((step * block, span_modes), lambda i: (i, 0))
+    hbm = pl.BlockSpec(memory_space=pl.ANY)
+    vmem = pl.BlockSpec(memory_space=pltpu.VMEM)
+    grid = (col_count, 3, 2, 2 * block, stream_local)
     return pl.pallas_call(
-        functools.partial(inverse_kernel, group, span_modes),
-        grid=(col_count // step,),
-        in_specs=[whole(x), whole(stream_wave), whole(split), table, table],
-        out_specs=pl.BlockSpec(
-            (step, 3, 2, 2 * block, stream_local), lambda i: (i, 0, 0, 0, 0)
+        start_kernel,
+        in_specs=[hbm] * 2 + [vmem] * 4,
+        out_specs=[hbm] * 2,
+        out_shape=[jax.ShapeDtypeStruct(grid, BF)] * 2,
+        scratch_shapes=[
+            pltpu.VMEM(a.shape, BF),
+            pltpu.VMEM(b.shape, BF),
+            pltpu.VMEM((span_modes, 6 * stream_local), BF),
+            pltpu.VMEM((2,) + grid, BF),
+            pltpu.SemaphoreType.DMA((2, rows - 1)),
+            pltpu.SemaphoreType.DMA((2, rows - 1)),
+            pltpu.SemaphoreType.DMA((2, col_count // 2, 2)),
+            pltpu.SemaphoreType.DMA((2, col_count // 2, 2)),
+            pltpu.SemaphoreType.DMA((2, 2)),
+        ],
+        compiler_params=pltpu.CompilerParams(
+            collective_id=1, has_side_effects=True, vmem_limit_bytes=VMEM_LIMIT
         ),
-        out_shape=jax.ShapeDtypeStruct((col_count, 3, 2, 2 * block, stream_local), BF),
-        scratch_shapes=[pltpu.VMEM((span_modes, 6 * stream_local), BF)],
-        compiler_params=pltpu.CompilerParams(vmem_limit_bytes=VMEM_LIMIT),
         cost_estimate=pl.CostEstimate(
-            flops=2 * 12 * stream_local * span_modes * half_points,
-            bytes_accessed=4 * half_points * span_modes + 4 * x.size,
+            flops=2 * 24 * stream_local * span_modes * half_points,
+            bytes_accessed=4 * half_points * span_modes + 4 * (a.size + b.size),
             transcendentals=0,
         ),
-        name="inverse_span",
-    )(x, stream_wave, split, cosine, sine)
+        name="start",
+    )(a, b, stream_wave, split, cosine, sine)
 
 
 def product_kernel(chunk, ga, gb, wave_c, wave_s, back_c, back_s, o0, o1, o2, reals, imags, acc_re, acc_im):
@@ -364,10 +445,6 @@
     )(*terms, split, cosine, sine)
 
 
-def exchange(x, axis):
-    return lax.all_to_all(x, axis, split_axis=0, concat_axis=0, tiled=True)
-
-
 def on_device(coefficients, basis_values, basis_slopes, band_offsets):
     row_count = lax.axis_size("row")
     col_count = lax.axis_size("col")
@@ -391,11 +468,7 @@
     stream_wave = (stream_index.astype(F32) * stream_unit)[None, :]
 
     sent = collocate(coefficients, basis_values, basis_slopes, band_offsets, 32)
-    grids = []
-    for group in range(2):
-        modes = exchange(sent[group], "row")
-        grid = inverse_span(group, modes, stream_wave, split, *span, col_count)
-        grids.append(exchange(grid, "col"))
+    grids = start(sent, stream_wave, split, *span, col_count)
     half = span_points // 2 // col_count
     terms = products(*grids, stream, 48 if half % 48 == 0 else half, 512)
     return finish(terms, split, *back, norm, row_count).astype(F32)

time: 306 us -> 253 us (0.83)
  Pallas kernels: 130 us -> 245 us
  blocking collectives: 89.9 us -> 0 us
  waiting for transfers between devices: 69.6 us -> 0 us
  starting transfers between devices: 7.35 us -> 0 us
    pallas_call x2 -> x1, Pallas kernels: 24.9 us -> 127 us  [start(): pl.pallas_call(start_kernel, in_specs=[hbm] * 2 + [vmem] * 4, out_specs=[...]
    all_to_all x2 -> x0, blocking collectives: 89.9 us -> none  [exchange(): return lax.all_to_all(x, axis, split_axis=0, concat_axis=0, tiled=True)]
    all_to_all x2 -> x0, waiting for transfers between devices: 69.6 us -> none  [exchange(): return lax.all_to_all(x, axis, split_axis=0, concat_axis=0, tiled=True)]
    pallas_call x1, Pallas kernels: 72 us -> 84.8 us  [finish(): pl.pallas_call(functools.partial(finish_kernel, norm), in_specs=[hbm] * 3...]
    all_to_all x2 -> x0, starting transfers between devices: 7.35 us -> none  [exchange(): return lax.all_to_all(x, axis, split_axis=0, concat_axis=0, tiled=True)]
  transfers between devices with their start and end apart: 2 -> 0, of which waited for: 2 -> 0; matrix products, arithmetic and copies ran while one was open for 0% -> 0% of each run, Pallas kernels for 8% -> 0%
where the time goes in v3:
time: 253 us; the launch traced here: 250 us
  Pallas kernels  245 us (97%)
  other arithmetic  4.8 us (2%)
    pallas_call x1, Pallas kernels, start(): pl.pallas_call(start_kernel, in_specs=[hbm] * 2 + [vmem] * 4, out_specs=[...  127 us
    pallas_call x1, Pallas kernels, finish(): pl.pallas_call(functools.partial(finish_kernel, norm), in_specs=[hbm] * 3...  84.8 us
    pallas_call x1, Pallas kernels, products(): pl.pallas_call(functools.partial(product_kernel, chunk), grid=(half // hb...  26.8 us
    pallas_call x1, Pallas kernels, collocate(): pl.pallas_call(collocate_kernel, grid=(stream_local // rows,), in_specs=[...  6.51 us

profile of v3, /device:TPU:0, one launch (start us, length us, event | category | flops | bytes accessed | tf_op | source)
XLA Modules:
  0.0 249.7 jit_solution(11193927300642176070)
XLA Ops:
  0.0 0.5 convert_multiply_fusion.stream_wave
  0.5 6.5 %collocate.1 = (bf16[4,2,128,768]{3,2,1,0:T(8,128)(2,1)}, bf16[4,3,128,768]{3,2,1,0:T(8,128)(2,1)}) custom-call(f32[4,4]{1,0:T(4,128)} %values.1, f32[4,4]{1,0:T(4,128)} %slopes.1, s32[4]{0:T(128)} %offsets.1, f32[3,7,128,768]{3,2,1,0:T(8,128)} %coef.1), custom_call_target="tpu_custom_call" | custom-call | tf_op jit(solution)/shard_map/collocate/pallas_call | solution.py:68
  7.0 126.8 %start.1 = (bf16[8,3,2,288,128]{4,3,2,1,0:T(8,128)(2,1)}, bf16[8,3,2,288,128]{4,3,2,1,0:T(8,128)(2,1)}) custom-call(bf16[4,2,128,768]{3,2,1,0:T(8,128)(2,1)} %get-tuple-element.12.a, bf16[4,3,128,768]{3,2,1,0:T(8,128)(2,1)} %get-tuple-element.13.b, f32[1,128]{1,0:T(1,128)} %convert_multiply_fusion.stream_wave, bf16[768,768]{1,0:T(8,128)(2,1)} %constant.30.clone.split, ...), custom_call_target="tpu_custom_call" | custom-call | flops 10871635968 | bytes 14942208 | tf_op jit(solution)/shard_map/start/pallas_call | solution.py:225
  133.8 26.8 %products.1 = (bf16[8,2,2,144,128]{4,3,2,1,0:T(8,128)(2,1)}, bf16[8,2,2,144,128]{4,3,2,1,0:T(8,128)(2,1)}, bf16[8,2,2,144,128]{4,3,2,1,0:T(8,128)(2,1)}) custom-call(bf16[8,3,2,2,144,128]{5,4,3,2,1,0:T(8,128)(2,1)} %bitcast.2, bf16[8,3,2,2,144,128]{5,4,3,2,1,0:T(8,128)(2,1)} %bitcast.3, bf16[1024,1536]{1,0:T(8,128)(2,1)} %constant.26.clone.wave_c, ...), custom_call_target="tpu_custom_call" | custom-call | flops 16307453952 | bytes 33816576 | tf_op jit(solution)/shard_map/products/pallas_call | solution.py:307
  160.6 84.8 %finish.1 = bf16[3,4,128,768]{3,2,1,0:T(8,128)(2,1)} custom-call(bf16[8,2,2,144,128]{4,3,2,1,0:T(8,128)(2,1)} %get-tuple-element.16.t0, bf16[8,2,2,144,128]{4,3,2,1,0:T(8,128)(2,1)} %get-tuple-element.17.t1, bf16[8,2,2,144,128]{4,3,2,1,0:T(8,128)(2,1)} %get-tuple-element.18.t2, bf16[768,768]{1,0:T(8,128)(2,1)} %constant.30.clone.split, ...), custom_call_target="tpu_custom_call" | custom-call | flops 5435817984 | bytes 21233664 | tf_op jit(solution)/shard_map/finish/pallas_call | solution.py:420
  245.4 4.3 %convert_element_type.14 = f32[3,4,128,768]{3,2,1,0:T(8,128)} convert(bf16[3,4,128,768]{3,2,1,0:T(8,128)(2,1)} %finish.1) | non-fusion elementwise | flops 1179648 | bytes 7077888 | tf_op jit(solution)/shard_map/convert_element_type | solution.py:474
